TPU v7x, 32 devices: a whole 2x2x4 slice. The times are simulated.
32 devices in a mesh: gx: 4 (over z), gy: 4 (over x, core), gz: 2 (over y).
Axes of the slice: x: 2, y: 2, z: 4, core: 2. Of those that a mesh axis runs over, the one named last changes fastest.
Arguments:
- right_side: float32 [64, 256, 512], P('gx', 'gy', 'gz'), may hold values from -4 to 4
- initial_guess: float32 [64, 256, 512], P('gx', 'gy', 'gz'), may hold values from -3 to 3
- damping: float32 [64, 256, 512], P('gx', 'gy', 'gz'), may hold values from 0.1 to 4
- group_map: int32 [16, 64, 128], P('gx', 'gy', 'gz'), may hold values from 0 to 1023
- block_inverse: float32 [1024, 1024], P('gy'), may hold values from -0.1875 to 0.1875
Outputs:
- fine_iterate: float32 [64, 256, 512], P('gx', 'gy', 'gz')
- middle_correction: float32 [32, 128, 256], P('gx', 'gy', 'gz')
- coarse_correction: float32 [16, 64, 128], P('gx', 'gy', 'gz')
- aggregate_solution: float32 [1024], P('gy')
All inputs are finite; a program needn't handle non-finite values.
Results may differ from a plain program's by a relative error of at most 0.0003.
Values sent between devices are 32-bit elements; how exact they have to be, the bound alone decides.
A program may use at most 192 MiB of HBM per device.

v0:
```python
import math

import jax
import jax.numpy as jnp
from jax import lax
from jax.sharding import PartitionSpec as P

SWEEPS = 4
NAGG = 1024


OMEGA = 0.8


def with_halo(cells, sides, width):
    for axis, dim in sides:
        count = lax.axis_size(axis)
        ends = count - 1
        head = lax.slice_in_dim(cells, 0, width, axis=dim)
        tail = lax.slice_in_dim(cells, cells.shape[dim] - width, cells.shape[dim], axis=dim)
        cells = jnp.concatenate(
            [
                lax.ppermute(tail, axis, [(i, (i + 1) % count) for i in range(ends)]),
                cells,
                lax.ppermute(head, axis, [((i + 1) % count, i) for i in range(ends)]),
            ],
            axis=dim,
        )
    return cells


def neighbours(padded):
    total = padded[2:, 1:-1, 1:-1] + padded[:-2, 1:-1, 1:-1]
    total = total + padded[1:-1, 2:, 1:-1] + padded[1:-1, :-2, 1:-1]
    return total + padded[1:-1, 1:-1, 2:] + padded[1:-1, 1:-1, :-2]


def relax(padded, source, diagonal):
    centre = padded[1:-1, 1:-1, 1:-1]
    return centre + OMEGA * (source - (diagonal * centre - neighbours(padded))) / diagonal


def defect(padded, source, diagonal):
    centre = padded[1:-1, 1:-1, 1:-1]
    return source - (diagonal * centre - neighbours(padded))


def shrink(field):
    extent_a, extent_b, extent_c = field.shape
    blocks = field.reshape(extent_a // 2, 2, extent_b // 2, 2, extent_c // 2, 2)
    return blocks.sum(axis=(1, 3, 5)) * 0.125


def fine_rim(field):
    return with_halo(field, (("gx", 0), ("gy", 1), ("gz", 2)), 1)


def middle_rim(field):
    return with_halo(field, (("gx", 0), ("gy", 1), ("gz", 2)), 1)


def coarse_rim(field):
    return with_halo(field, (("gx", 0), ("gy", 1), ("gz", 2)), 1)


def shards(right_side, initial_guess, damping, group_map, block_inverse):
    fine_diag = 6.0 + damping
    iterate = initial_guess
    for sweep_count in range(SWEEPS):
        iterate = relax(fine_rim(iterate), right_side, fine_diag)
    fine_defect = defect(fine_rim(iterate), right_side, fine_diag)
    middle_damp = 4.0 * shrink(damping)
    middle_source = 4.0 * shrink(fine_defect)
    middle_diag = 6.0 + middle_damp
    middle = OMEGA * middle_source / middle_diag
    for sweep_count in range(SWEEPS - 1):
        middle = relax(middle_rim(middle), middle_source, middle_diag)
    middle_defect = defect(middle_rim(middle), middle_source, middle_diag)
    coarse_damp = 4.0 * shrink(middle_damp)
    coarse_source = 4.0 * shrink(middle_defect)
    coarse_diag = 6.0 + coarse_damp
    coarse = OMEGA * coarse_source / coarse_diag
    for sweep_count in range(SWEEPS - 1):
        coarse = relax(coarse_rim(coarse), coarse_source, coarse_diag)
    coarse_defect = defect(coarse_rim(coarse), coarse_source, coarse_diag)
    partial_sums = jax.ops.segment_sum(
        coarse_defect.reshape(-1), group_map.reshape(-1), num_segments=NAGG
    )
    summed = lax.psum(partial_sums, ("gx", "gy", "gz"))
    group_cells = (
        coarse_source.size * lax.axis_size("gx") * lax.axis_size("gy") * lax.axis_size("gz") // NAGG
    )
    aggregate_source = summed / math.sqrt(group_cells)
    solution = jnp.dot(block_inverse, aggregate_source, precision=lax.Precision.HIGHEST)
    return (iterate, middle, coarse, solution)


def solution(mesh):
    return jax.shard_map(
        shards,
        mesh=mesh,
        in_specs=(
            P("gx", "gy", "gz"),
            P("gx", "gy", "gz"),
            P("gx", "gy", "gz"),
            P("gx", "gy", "gz"),
            P("gy", None),
        ),
        out_specs=(P("gx", "gy", "gz"), P("gx", "gy", "gz"), P("gx", "gy", "gz"), P("gy")),
        check_vma=False,
    )
```

profile of v0, /device:TPU:0, one launch (start us, length us, event | category | flops | bytes accessed | tf_op | source)
XLA Modules:
  0.0 751.2 jit_solution(6670065495975594956)
XLA Ops:
  1.6 4.9 collective-permute-start.1
  8.4 4.3 collective-permute-done
  28.2 4.5 collective-permute-start.5
  47.8 21.0 %fusion.42 = f32[16,64,256]{1,0,2:T(8,128)S(1)} fusion(f32[16,64,256]{1,0,2:T(8,128)} %copy.173, f32[16,64,256]{1,0,2:T(8,128)} %copy.172, f32[18,66,1]{1,0,2:T(8,128)S(1)} %collective-permute-done.5, f32[18,1,256]{1,0,2:T(8,128)} %copy.165, f32[18,64,256]{1,0,2:T(8,128)} %copy.164, f32[18,1,256]{1,0,2:T(8,128)} %copy.167, ...), kind=kLoop, calls=%fused_computation.120 | loop fusion | flops 5242880 | bytes 7517472 | tf_op jit(solution)/shard_map/add | solution.py:40
  71.9 4.5 collective-permute-start.7
  103.3 4.5 collective-permute-start.11
  109.2 10.2 %fusion.32 = f32[16,64,256]{1,0,2:T(8,128)S(1)} fusion(f32[16,64,256]{1,0,2:T(8,128)S(1)} %copy-done.7, f32[16,64,256]{1,0,2:T(8,128)S(1)} %copy-done.1, f32[18,66,1]{1,0,2:T(8,128)S(1)} %collective-permute-done.11, f32[18,1,256]{1,0,2:T(8,128)} %copy.181, f32[18,1,256]{1,0,2:T(8,128)S(1)} %copy-done.12, f32[1,64,256]{1,0,2:T(1,128)S(1)} %copy.175, ...), kind=kLoop, calls=%fused_computation.92 | loop fusion | flops 7864320 | bytes 4371744 | tf_op jit(solution)/shard_map/add | solution.py:40
  122.4 4.9 collective-permute-start.13
  152.4 4.5 collective-permute-start.17
  158.4 10.2 %fusion.22 = f32[16,64,256]{1,0,2:T(8,128)S(1)} fusion(f32[16,64,256]{1,0,2:T(8,128)S(1)} %copy-done.9, f32[16,64,256]{1,0,2:T(8,128)S(1)} %copy-done.2, f32[18,66,1]{1,0,2:T(8,128)S(1)} %collective-permute-done.17, f32[18,1,256]{1,0,2:T(8,128)} %copy.194, f32[18,1,256]{1,0,2:T(8,128)S(1)} %copy-done.13, f32[1,64,256]{1,0,2:T(1,128)S(1)} %copy.188, ...), kind=kLoop, calls=%fused_computation.64 | loop fusion | flops 7864320 | bytes 4371744 | tf_op jit(solution)/shard_map/add | solution.py:40
  171.6 5.1 collective-permute-start.19
  201.6 4.5 collective-permute-start.23
  207.6 10.2 %fusion.12 = f32[16,64,256]{1,0,2:T(8,128)S(1)} fusion(f32[16,64,256]{1,0,2:T(8,128)S(1)} %copy-done.11, f32[16,64,256]{1,0,2:T(8,128)S(1)} %copy-done.3, f32[18,66,1]{1,0,2:T(8,128)S(1)} %collective-permute-done.23, f32[18,1,256]{1,0,2:T(8,128)} %copy.207, f32[18,1,256]{1,0,2:T(8,128)S(1)} %copy-done.14, f32[1,64,256]{1,0,2:T(1,128)S(1)} %copy.201, ...), kind=kLoop, calls=%fused_computation.36 | loop fusion | flops 7864320 | bytes 4371744 | tf_op jit(solution)/shard_map/add | solution.py:40
  221.3 4.9 collective-permute-start.25
  251.9 5.3 collective-permute-start.29
  257.2 69.2 %reshape.25 = f32[8,2,32,2,128,2]{5,4,3,2,1,0:T(8,128)} reshape(f32[16,64,256]{2,1,0:T(8,128)} %param.7) | data formatting | bytes 2097152 | tf_op jit(solution)/shard_map/reshape | solution.py:50
  326.4 20.8 %reduce_sum.37 = f32[8,32,128]{2,1,0:T(8,128)S(1)} reduce(f32[8,2,32,2,128,2]{5,4,3,2,1,0:T(8,128)} %reshape.25, f32[]{:T(128)} %constant.9.clone.1), dimensions={1,3,5}, to_apply=%region_1.0 | reduce | flops 229376 | bytes 1179652 | tf_op jit(solution)/shard_map/reduce_sum | solution.py:51
  347.2 23.0 %fusion.2 = f32[16,64,256]{1,0,2:T(8,128)} fusion(f32[16,64,256]{1,0,2:T(8,128)} %copy.172, f32[18,66,1]{1,0,2:T(8,128)} %collective-permute-done.29, f32[18,1,256]{1,0,2:T(8,128)} %copy.220, f32[18,1,256]{1,0,2:T(8,128)} %copy.222, f32[1,64,256]{1,0,2:T(1,128)S(1)} %copy.214, f32[16,64,256]{1,0,2:T(8,128)} %copy-done.4, f32[1,64,256]{1,0,2:T(1,128)S(1)} %copy.216, ...), kind=kLoop, calls=%fused_computation.8 | loop fusion | flops 7077888 | bytes 4371744 | tf_op jit(solution)/shard_map/sub | solution.py:45
  372.7 68.4 %reshape.24 = f32[8,2,32,2,128,2]{5,4,3,2,1,0:T(8,128)} reshape(f32[16,64,256]{2,1,0:T(8,128)S(1)} %copy.226) | data formatting | bytes 2097152 | tf_op jit(solution)/shard_map/reshape | solution.py:50
  441.0 20.8 %reduce_sum.36 = f32[8,32,128]{2,1,0:T(8,128)S(1)} reduce(f32[8,2,32,2,128,2]{5,4,3,2,1,0:T(8,128)} %reshape.24, f32[]{:T(128)} %constant.9.clone.1), dimensions={1,3,5}, to_apply=%region_0.0 | reduce | flops 229376 | bytes 1179652 | tf_op jit(solution)/shard_map/reduce_sum | solution.py:51
  480.9 4.6 collective-permute-start.35
  506.9 4.6 collective-permute-start.41
  532.8 4.6 collective-permute-start.47
  556.8 4.8 collective-permute-start.53
  561.6 9.8 %mul.126 = f32[4,2,16,2,64,2]{5,4,3,2,1,0:T(8,128)} reshape(f32[8,32,128]{2,1,0:T(8,128)S(1)} %get-tuple-element.65) | data formatting | bytes 262144 | tf_op jit(solution)/shard_map/mul | solution.py:72
  575.6 9.8 %reshape.26 = f32[4,2,16,2,64,2]{5,4,3,2,1,0:T(8,128)} reshape(f32[8,32,128]{2,1,0:T(8,128)S(1)} %fusion.48) | data formatting | bytes 262144 | tf_op jit(solution)/shard_map/reshape | solution.py:50
  605.4 4.5 collective-permute-start.59
  627.8 4.5 collective-permute-start.65
  650.2 4.5 collective-permute-start.71
  673.2 4.5 collective-permute-start.77
  680.2 28.8 %scatter_custom_fusion = f32[1024]{0:T(1024)S(1)} fusion(s32[4096]{0:T(1024)S(1)} %reshape.30, f32[4096]{0:T(1024)S(1)} %reshape.32, f32[]{:T(128)} %constant.9.clone.1), kind=kCustom, calls=%fused_computation.414 | custom fusion | flops 4096 | bytes 4100 | tf_op jit(solution)/shard_map/scatter-add | solution.py:86
  709.0 40.3 %psum.7 = f32[1024]{0:T(1024)S(1)} all-reduce(f32[1024]{0:T(1024)S(1)} %scatter_custom_fusion), channel_id=1, replica_groups=mesh['gx'=4,'gy'=4,'gz'=2] {'gx','gy','gz'}, use_global_device_ids=true, to_apply=%region_5.0 | all-reduce | flops 1024 | bytes 8192 | tf_op jit(solution)/shard_map/psum | solution.py:89
  (291 shorter events, 317.8 us)
Async XLA Ops:
  1.6 6.8 collective-permute-start.1
  26.8 21.0 %collective-permute-start.4 = (f32[18,66,1]{1,0,2:T(8,128)S(1)}, f32[18,66,1]{1,0,2:T(8,128)S(1)}, u32[]{:S(2)}, u32[]{:S(2)}) collective-permute-start(f32[18,66,1]{1,0,2:T(8,128)S(1)} %get-tuple-element.16), channel_id=1, source_target_pairs={{1,0},{3,2},{5,4},{7,6},{9,8},{11,10},{13,12},{15,14},{17,16},{19,... | collective-permute-start | bytes 14264 | tf_op jit(solution)/shard_map/ppermute | solution.py:25
  28.2 19.6 %collective-permute-start.5 = (f32[18,66,1]{1,0,2:T(8,128)S(1)}, f32[18,66,1]{1,0,2:T(8,128)S(1)}, u32[]{:S(2)}, u32[]{:S(2)}) collective-permute-start(f32[18,66,1]{1,0,2:T(8,128)S(1)} %get-tuple-element.17), channel_id=1, source_target_pairs={{0,1},{2,3},{4,5},{6,7},{8,9},{10,11},{12,13},{14,15},{16,17},{18,... | collective-permute-start | bytes 14264 | tf_op jit(solution)/shard_map/ppermute | solution.py:23
  70.5 6.2 collective-permute-start.6
  71.9 6.4 collective-permute-start.7
  86.6 7.2 collective-permute-start.9
  121.1 6.5 collective-permute-start.12
  122.4 7.0 collective-permute-start.13
  170.2 6.5 collective-permute-start.18
  171.6 6.8 collective-permute-start.19
  186.7 6.2 collective-permute-start.21
  219.3 6.9 collective-permute-start.24
  221.3 7.1 collective-permute-start.25
  236.7 6.2 collective-permute-start.27
  250.6 96.6 %collective-permute-start.28 = (f32[18,66,1]{1,0,2:T(8,128)}, f32[18,66,1]{1,0,2:T(8,128)S(1)}, u32[]{:S(2)}, u32[]{:S(2)}) collective-permute-start(f32[18,66,1]{1,0,2:T(8,128)} %get-tuple-element.18), channel_id=1, source_target_pairs={{1,0},{3,2},{5,4},{7,6},{9,8},{11,10},{13,12},{15,14},{17,16},{19,... | collective-permute-start | bytes 14264 | tf_op jit(solution)/shard_map/ppermute | solution.py:25
  251.9 95.3 %collective-permute-start.29 = (f32[18,66,1]{1,0,2:T(8,128)}, f32[18,66,1]{1,0,2:T(8,128)}, u32[]{:S(2)}, u32[]{:S(2)}) collective-permute-start(f32[18,66,1]{1,0,2:T(8,128)} %get-tuple-element.19), channel_id=1, source_target_pairs={{0,1},{2,3},{4,5},{6,7},{8,9},{10,11},{12,13},{14,15},{16,17},{18,... | collective-permute-start | bytes 14264 | tf_op jit(solution)/shard_map/ppermute | solution.py:23
  479.6 8.4 %collective-permute-start.34 = (f32[10,34,1]{2,1,0:T(8,128)S(1)}, f32[10,34,1]{2,1,0:T(8,128)S(1)}, u32[]{:S(2)}, u32[]{:S(2)}) collective-permute-start(f32[10,34,1]{2,1,0:T(8,128)S(1)} %get-tuple-element.55), channel_id=1, source_target_pairs={{1,0},{3,2},{5,4},{7,6},{9,8},{11,10},{13,12},{15,14},{17,16},{19,... | collective-permute-start | bytes 4088 | tf_op jit(solution)/shard_map/ppermute | solution.py:25
  480.9 8.9 %collective-permute-start.35 = (f32[10,34,1]{2,1,0:T(8,128)S(1)}, f32[10,34,1]{2,1,0:T(8,128)S(1)}, u32[]{:S(2)}, u32[]{:S(2)}) collective-permute-start(f32[10,34,1]{2,1,0:T(8,128)S(1)} %get-tuple-element.56), channel_id=1, source_target_pairs={{0,1},{2,3},{4,5},{6,7},{8,9},{10,11},{12,13},{14,15},{16,17},{18,... | collective-permute-start | bytes 4088 | tf_op jit(solution)/shard_map/ppermute | solution.py:23
  505.6 8.2 %collective-permute-start.40 = (f32[10,34,1]{2,1,0:T(8,128)S(1)}, f32[10,34,1]{2,1,0:T(8,128)S(1)}, u32[]{:S(2)}, u32[]{:S(2)}) collective-permute-start(f32[10,34,1]{2,1,0:T(8,128)S(1)} %get-tuple-element.53), channel_id=1, source_target_pairs={{1,0},{3,2},{5,4},{7,6},{9,8},{11,10},{13,12},{15,14},{17,16},{19,... | collective-permute-start | bytes 4088 | tf_op jit(solution)/shard_map/ppermute | solution.py:25
  506.9 8.7 %collective-permute-start.41 = (f32[10,34,1]{2,1,0:T(8,128)S(1)}, f32[10,34,1]{2,1,0:T(8,128)S(1)}, u32[]{:S(2)}, u32[]{:S(2)}) collective-permute-start(f32[10,34,1]{2,1,0:T(8,128)S(1)} %get-tuple-element.54), channel_id=1, source_target_pairs={{0,1},{2,3},{4,5},{6,7},{8,9},{10,11},{12,13},{14,15},{16,17},{18,... | collective-permute-start | bytes 4088 | tf_op jit(solution)/shard_map/ppermute | solution.py:23
  531.5 8.2 %collective-permute-start.46 = (f32[10,34,1]{2,1,0:T(8,128)S(1)}, f32[10,34,1]{2,1,0:T(8,128)S(1)}, u32[]{:S(2)}, u32[]{:S(2)}) collective-permute-start(f32[10,34,1]{2,1,0:T(8,128)S(1)} %get-tuple-element.51), channel_id=1, source_target_pairs={{1,0},{3,2},{5,4},{7,6},{9,8},{11,10},{13,12},{15,14},{17,16},{19,... | collective-permute-start | bytes 4088 | tf_op jit(solution)/shard_map/ppermute | solution.py:25
  532.8 8.7 %collective-permute-start.47 = (f32[10,34,1]{2,1,0:T(8,128)S(1)}, f32[10,34,1]{2,1,0:T(8,128)S(1)}, u32[]{:S(2)}, u32[]{:S(2)}) collective-permute-start(f32[10,34,1]{2,1,0:T(8,128)S(1)} %get-tuple-element.52), channel_id=1, source_target_pairs={{0,1},{2,3},{4,5},{6,7},{8,9},{10,11},{12,13},{14,15},{16,17},{18,... | collective-permute-start | bytes 4088 | tf_op jit(solution)/shard_map/ppermute | solution.py:23
  555.5 19.9 %collective-permute-start.52 = (f32[10,34,1]{2,1,0:T(8,128)S(1)}, f32[10,34,1]{2,1,0:T(8,128)S(1)}, u32[]{:S(2)}, u32[]{:S(2)}) collective-permute-start(f32[10,34,1]{2,1,0:T(8,128)S(1)} %get-tuple-element.49), channel_id=1, source_target_pairs={{1,0},{3,2},{5,4},{7,6},{9,8},{11,10},{13,12},{15,14},{17,16},{19,... | collective-permute-start | bytes 4088 | tf_op jit(solution)/shard_map/ppermute | solution.py:25
  556.8 18.6 %collective-permute-start.53 = (f32[10,34,1]{2,1,0:T(8,128)S(1)}, f32[10,34,1]{2,1,0:T(8,128)S(1)}, u32[]{:S(2)}, u32[]{:S(2)}) collective-permute-start(f32[10,34,1]{2,1,0:T(8,128)S(1)} %get-tuple-element.50), channel_id=1, source_target_pairs={{0,1},{2,3},{4,5},{6,7},{8,9},{10,11},{12,13},{14,15},{16,17},{18,... | collective-permute-start | bytes 4088 | tf_op jit(solution)/shard_map/ppermute | solution.py:23
  604.1 6.2 collective-permute-start.58
  605.4 6.5 collective-permute-start.59
  626.5 6.2 collective-permute-start.64
  627.8 6.5 collective-permute-start.65
  648.9 6.2 collective-permute-start.70
  650.2 6.5 collective-permute-start.71
  671.9 7.9 %collective-permute-start.76 = (f32[6,18,1]{2,1,0:T(8,128)}, f32[6,18,1]{2,1,0:T(8,128)S(1)}, u32[]{:S(2)}, u32[]{:S(2)}) collective-permute-start(f32[6,18,1]{2,1,0:T(8,128)} %get-tuple-element.75), channel_id=1, source_target_pairs={{1,0},{3,2},{5,4},{7,6},{9,8},{11,10},{13,12},{15,14},{17,16},{19,... | collective-permute-start | bytes 1304 | tf_op jit(solution)/shard_map/ppermute | solution.py:25
  673.2 6.8 collective-permute-start.77
  (66 other events, 1372.7 us)
where the time goes:
time: 762 us; the launch traced here: 751 us
  local copies, waits for them, and re-layouts  245 us (32%)
  starting transfers between devices  187 us (25%)
  other arithmetic  172 us (23%)
  waiting for transfers between devices  103 us (14%)
  blocking collectives  40.3 us (5%)
    reshape x3, local copies, waits for them, and re-layouts, shrink(): blocks = field.reshape(extent_a // 2, 2, extent_b // 2, 2, extent_c // 2, 2)  147 us
    ppermute x39, starting transfers between devices, with_halo(): lax.ppermute(tail, axis, [(i, (i + 1) % count) for i in range(ends)])  136 us
    ppermute x39, waiting for transfers between devices, with_halo(): lax.ppermute(head, axis, [((i + 1) % count, i) for i in range(ends)])  79.7 us
    add x10, other arithmetic, relax(): centre + OMEGA * (source - (diagonal * centre - neighbours(padded))) / di...  52.4 us
    ppermute x39, starting transfers between devices, with_halo(): lax.ppermute(head, axis, [((i + 1) % count, i) for i in range(ends)])  51.3 us
    reduce_sum x4, other arithmetic, shrink(): return blocks.sum(axis=(1, 3, 5)) * 0.125  49.6 us
    psum x1, blocking collectives, shards(): summed = lax.psum(partial_sums, ('gx', 'gy', 'gz'))  40.3 us
    scatter-add x1, other arithmetic, shards(): jax.ops.segment_sum(coarse_defect.reshape(-1), group_map.reshape(-1), num...  28.8 us
  transfers between devices with their start and end apart: 78, of which 48 were waited for; matrix products, arithmetic and copies ran while one was open for 19% of the time, Pallas kernels for 0%

commit v1 on v0

v1 whole, which is shorter than its diff:
```python
import functools
import math

import jax
import jax.numpy as jnp
from jax import lax
from jax.experimental import pallas as pl
from jax.experimental.pallas import tpu as pltpu
from jax.sharding import PartitionSpec as P

SWEEPS = 4
NAGG = 1024
OMEGA = 0.8
LANES = 128
MESH = pl.DeviceIdType.MESH


def split_dot(left, right_bf16, dims):
    high = left.astype(jnp.bfloat16)
    low = (left - high.astype(jnp.float32)).astype(jnp.bfloat16)
    out = lax.dot_general(high, right_bf16, dims, preferred_element_type=jnp.float32)
    return out + lax.dot_general(low, right_bf16, dims, preferred_element_type=jnp.float32)


def pair_matrix(rows, columns):
    row = lax.broadcasted_iota(jnp.int32, (rows, columns), 0)
    column = lax.broadcasted_iota(jnp.int32, (rows, columns), 1)
    first = jnp.where(row == 2 * column, 1.0, 0.0)
    return (first + jnp.where(row == 2 * column + 1, 1.0, 0.0)).astype(jnp.bfloat16)


class Level:
    def __init__(self, dims, lanes, fields, y_send, y_recv, z_send, z_recv, sems, place, counts):
        self.nx, self.ny, self.nz = dims
        self.lanes = lanes
        self.fields, self.y_send, self.y_recv = fields, y_send, y_recv
        self.z_send, self.z_recv = z_send, z_recv
        self.send_sem, self.recv_sem = sems
        self.gx, self.gy, self.gz = place
        self.counts = counts
        self.edge = jnp.where(self.gz == 0, self.nz - 1, 0)

    def clear(self):
        nx, ny, lanes = self.nx, self.ny, self.lanes
        rounds = self.fields.shape[0]

        @pl.when(self.gx == 0)
        def _():
            for step in range(rounds):
                self.fields[step, 0] = jnp.zeros((ny, lanes), jnp.float32)

        @pl.when(self.gx == self.counts[0] - 1)
        def _():
            for step in range(rounds):
                self.fields[step, nx + 1] = jnp.zeros((ny, lanes), jnp.float32)

        @pl.when(self.gy == 0)
        def _():
            for step in range(rounds):
                self.y_recv[step, 0] = jnp.zeros((nx, lanes), jnp.float32)

        @pl.when(self.gy == self.counts[1] - 1)
        def _():
            for step in range(rounds):
                self.y_recv[step, 1] = jnp.zeros((nx, lanes), jnp.float32)

        for step in range(rounds):
            self.z_send[step] = jnp.zeros((ny, LANES), jnp.float32)

    def x_copies(self, step, low=None, high=None):
        gx, gy, gz = self.gx, self.gy, self.gz
        field = self.fields.at[step]
        low = field.at[1] if low is None else low
        high = field.at[self.nx] if high is None else high
        up = pltpu.make_async_remote_copy(
            src_ref=high, dst_ref=field.at[0],
            send_sem=self.send_sem.at[step, 0], recv_sem=self.recv_sem.at[step, 0],
            device_id=(gx + 1, gy, gz), device_id_type=MESH)
        down = pltpu.make_async_remote_copy(
            src_ref=low, dst_ref=field.at[self.nx + 1],
            send_sem=self.send_sem.at[step, 1], recv_sem=self.recv_sem.at[step, 1],
            device_id=(gx - 1, gy, gz), device_id_type=MESH)
        return (gx, self.counts[0], up, down)

    def y_copies(self, step):
        gx, gy, gz = self.gx, self.gy, self.gz
        up = pltpu.make_async_remote_copy(
            src_ref=self.y_send.at[step, 1], dst_ref=self.y_recv.at[step, 0],
            send_sem=self.send_sem.at[step, 2], recv_sem=self.recv_sem.at[step, 2],
            device_id=(gx, gy + 1, gz), device_id_type=MESH)
        down = pltpu.make_async_remote_copy(
            src_ref=self.y_send.at[step, 0], dst_ref=self.y_recv.at[step, 1],
            send_sem=self.send_sem.at[step, 3], recv_sem=self.recv_sem.at[step, 3],
            device_id=(gx, gy - 1, gz), device_id_type=MESH)
        return (gy, self.counts[1], up, down)

    def z_copy(self, step):
        return pltpu.make_async_remote_copy(
            src_ref=self.z_send.at[step], dst_ref=self.z_recv.at[step],
            send_sem=self.send_sem.at[step, 4], recv_sem=self.recv_sem.at[step, 4],
            device_id=(self.gx, self.gy, 1 - self.gz), device_id_type=MESH)

    @staticmethod
    def start(copies):
        at, count, up, down = copies
        pl.when(at < count - 1)(up.start)
        pl.when(at > 0)(down.start)

    @staticmethod
    def wait_recv(copies):
        at, count, up, down = copies
        pl.when(at > 0)(up.wait_recv)
        pl.when(at < count - 1)(down.wait_recv)

    @staticmethod
    def wait_send(copies):
        at, count, up, down = copies
        pl.when(at < count - 1)(up.wait_send)
        pl.when(at > 0)(down.wait_send)

    def start_yz(self, step):
        self.z_copy(step).start()
        self.start(self.y_copies(step))

    def start_all(self, step):
        self.start(self.x_copies(step))
        self.start_yz(step)

    def wait_yz(self, step):
        self.wait_recv(self.y_copies(step))
        self.z_copy(step).wait_recv()

    def wait_x(self, step):
        self.wait_recv(self.x_copies(step))

    def wait_sends(self, step):
        self.wait_send(self.x_copies(step))
        self.wait_send(self.y_copies(step))
        self.z_copy(step).wait_send()

    def pack(self, step, x, value):
        ny, lanes = self.ny, self.lanes
        self.y_send[step, 0, pl.ds(x, 1), :] = value[0:1]
        self.y_send[step, 1, pl.ds(x, 1), :] = value[ny - 1:ny]
        if lanes > LANES:
            tile = jnp.where(self.gz == 0, value[:, lanes - LANES:], value[:, :LANES])
        else:
            tile = value
        edge = lax.rem(self.edge, LANES)
        turned = pltpu.roll(tile, lax.rem(x - edge + LANES, LANES), 1)
        lane = lax.broadcasted_iota(jnp.int32, (ny, LANES), 1)
        self.z_send[step] = jnp.where(lane == x, turned, self.z_send[step])

    def around(self, step, x):
        ny, lanes = self.ny, self.lanes
        field = self.fields.at[step]
        value = field[x + 1]
        total = field[x] + field[x + 2]
        row = lax.broadcasted_iota(jnp.int32, (ny, lanes), 0)
        lane = lax.broadcasted_iota(jnp.int32, (ny, lanes), 1)
        below = self.y_recv[step, 0, pl.ds(x, 1), :]
        above = self.y_recv[step, 1, pl.ds(x, 1), :]
        total = total + jnp.where(row == 0, below, pltpu.roll(value, 1, 0))
        total = total + jnp.where(row == ny - 1, above, pltpu.roll(value, ny - 1, 0))
        total = total + jnp.where(lane == 0, 0.0, pltpu.roll(value, 1, 1))
        total = total + jnp.where(lane == lanes - 1, 0.0, pltpu.roll(value, lanes - 1, 1))
        edge = lax.rem(self.edge, LANES)
        face = pltpu.roll(self.z_recv[step], lax.rem(edge - x + LANES, LANES), 1)
        if lanes > LANES:
            face = jnp.concatenate([face] * (lanes // LANES), axis=1)
        return value, total + jnp.where(lane == self.edge, face, 0.0)


def kernel(counts, rhs_hbm, guess_hbm, damp_hbm, group_hbm, inverse_hbm,
           fine_hbm, middle_hbm, coarse_hbm, solved_ref,
           f_fields, f_ys, f_yr, f_zs, f_zr,
           m_fields, m_ys, m_yr, m_zs, m_zr,
           c_fields, c_ys, c_yr, c_zs, c_zr,
           rhs, damp, group, inverse, weight, scaled,
           m_damp, m_src, m_weight, m_scaled, c_damp, c_src, c_weight, c_scaled,
           halves, quarters, c_defect, c_out, group_rows, onehot, reduced, gathered,
           f_send, f_recv, m_send, m_recv, c_send, c_recv,
           r_send, r_recv, g_send, g_recv, local_sem):
    place = gx, gy, gz = lax.axis_index("gx"), lax.axis_index("gy"), lax.axis_index("gz")
    cx, cy, cz = counts
    bx, by, bz = rhs.shape
    fine = Level((bx, by, bz), bz, f_fields, f_ys, f_yr, f_zs, f_zr, (f_send, f_recv), place, counts)
    middle = Level((bx // 2, by // 2, bz // 2), bz // 2, m_fields, m_ys, m_yr, m_zs, m_zr,
                   (m_send, m_recv), place, counts)
    coarse = Level((bx // 4, by // 4, bz // 4), LANES, c_fields, c_ys, c_yr, c_zs, c_zr,
                   (c_send, c_recv), place, counts)

    loads = [
        pltpu.make_async_copy(guess_hbm, f_fields.at[0, pl.ds(1, bx)], local_sem.at[0]),
        pltpu.make_async_copy(damp_hbm, damp, local_sem.at[1]),
        pltpu.make_async_copy(rhs_hbm, rhs, local_sem.at[2]),
        pltpu.make_async_copy(group_hbm, group, local_sem.at[3]),
        pltpu.make_async_copy(inverse_hbm, inverse, local_sem.at[4]),
    ]
    for load in loads:
        load.start()

    mates = [(i, k) for i in range(cx) for k in range(cz)]
    barrier = pltpu.get_barrier_semaphore()
    for i, k in mates:
        @pl.when(jnp.logical_or(gx != i, gz != k))
        def _():
            pl.semaphore_signal(barrier, inc=1, device_id=(i, gy, k), device_id_type=MESH)
    for j in range(cy):
        @pl.when(gy != j)
        def _():
            pl.semaphore_signal(barrier, inc=1, device_id=(gx, j, gz), device_id_type=MESH)

    for level in (fine, middle, coarse):
        level.clear()
    pl.semaphore_wait(barrier, len(mates) - 1 + cy - 1)

    first_x = fine.x_copies(0, guess_hbm.at[0], guess_hbm.at[bx - 1])
    fine.start(first_x)
    loads[0].wait()

    @pl.loop(0, bx)
    def _(x):
        fine.pack(0, x, f_fields[0, x + 1])

    fine.start_yz(0)

    loads[1].wait()
    loads[2].wait()
    pair_fine = pair_matrix(bz, bz // 2)
    pair_middle = pair_matrix(bz // 2, LANES)

    @pl.loop(0, bx)
    def _(x):
        factor = OMEGA / (6.0 + damp[x])
        weight[x] = factor
        scaled[x] = factor * rhs[x]

    def shrink_to(source, target, scratch, pairs, nx, ny):
        for x in range(nx):
            both = source(2 * x) + source(2 * x + 1)
            scratch[pl.ds(x * 2 * ny, 2 * ny), :] = split_dot(both, pairs, (((1,), (0,)), ((), ())))
        for x in range(nx):
            even = scratch[pl.ds(x * 2 * ny, ny, stride=2), :]
            odd = scratch[pl.ds(x * 2 * ny + 1, ny, stride=2), :]
            target[x] = 0.5 * (even + odd)

    shrink_to(lambda x: damp[x], m_damp, halves, pair_fine, middle.nx, middle.ny)
    shrink_to(lambda x: m_damp[x], c_damp, quarters, pair_middle, coarse.nx, coarse.ny)
    c_lane = lax.broadcasted_iota(jnp.int32, (coarse.nx, coarse.ny, LANES), 2)
    m_weight[...] = OMEGA / (6.0 + m_damp[...])
    c_weight[...] = jnp.where(c_lane < coarse.nz, OMEGA / (6.0 + c_damp[...]), 0.0)

    loads[3].wait()
    rows = coarse.nx * coarse.ny
    cells = coarse.nz
    group_rows[...] = jnp.zeros((rows, LANES), jnp.int32)
    for x in range(coarse.nx):
        group_rows[pl.ds(x * coarse.ny, coarse.ny), pl.ds(0, cells)] = group[x]
    packed = group_rows[pl.ds(0, rows // 2), :]
    packed = packed + pltpu.roll(group_rows[pl.ds(rows // 2, rows // 2), :], cells, 1)
    group_rows[pl.ds(0, rows // 2), :] = packed
    half = rows // 4

    @pl.loop(0, half)
    def _(row):
        number = lax.broadcasted_iota(jnp.int32, (LANES, LANES), 0)
        for part in range(2):
            low = group_rows[pl.ds(row + part * half, 1), :] & (LANES - 1)
            onehot[row, :, part * LANES:(part + 1) * LANES] = jnp.where(
                number == low, 1.0, 0.0).astype(jnp.bfloat16)

    def sweep(level, step, weights, scaleds, planes, unroll=1):
        def one(x):
            value, total = level.around(step, x)
            new = (1.0 - OMEGA) * value + (scaleds[x] + weights[x] * total)
            level.fields[step + 1, x + 1] = new
            level.pack(step + 1, x, new)

        level.wait_yz(step)

        @pl.loop(1, planes - 1)
        def _(x):
            one(x)

        level.wait_x(step)
        one(0)
        one(planes - 1)
        level.start_all(step + 1)

    for step in range(SWEEPS):
        sweep(fine, step, weight, scaled, bx)
    store_fine = pltpu.make_async_copy(f_fields.at[SWEEPS, pl.ds(1, bx)], fine_hbm, local_sem.at[5])
    store_fine.start()

    fine.wait_yz(SWEEPS)

    def defect_pair(x):
        total = None
        for plane in (2 * x, 2 * x + 1):
            value, around = fine.around(SWEEPS, plane)
            part = rhs[plane] - ((6.0 + damp[plane]) * value - around)
            total = part if total is None else total + part
        halves[pl.ds(pl.multiple_of(x * by, by), by), :] = split_dot(total, pair_fine, (((1,), (0,)), ((), ())))

    @pl.loop(1, middle.nx - 1)
    def _(x):
        defect_pair(x)

    fine.wait_x(SWEEPS)
    defect_pair(0)
    defect_pair(middle.nx - 1)

    def enter(level, scratch, source, weights, scaleds):
        ny = level.ny
        for x in range(level.nx):
            even = scratch[pl.ds(x * 2 * ny, ny, stride=2), :]
            odd = scratch[pl.ds(x * 2 * ny + 1, ny, stride=2), :]
            source[x] = 0.5 * (even + odd)
            scaleds[x] = weights[x] * source[x]
            level.fields[0, x + 1] = scaleds[x]
            level.pack(0, x, scaleds[x])
        level.start_all(0)

    enter(middle, halves, m_src, m_weight, m_scaled)
    for step in range(SWEEPS - 1):
        sweep(middle, step, m_weight, m_scaled, middle.nx)
    last = SWEEPS - 1
    store_middle = pltpu.make_async_copy(m_fields.at[last, pl.ds(1, middle.nx)], middle_hbm, local_sem.at[6])
    store_middle.start()
    middle.wait_yz(last)
    middle.wait_x(last)

    my = middle.ny
    for x in range(coarse.nx):
        total = None
        for plane in (2 * x, 2 * x + 1):
            value, around = middle.around(last, plane)
            part = m_src[plane] - ((6.0 + m_damp[plane]) * value - around)
            total = part if total is None else total + part
        quarters[pl.ds(x * my, my), :] = split_dot(total, pair_middle, (((1,), (0,)), ((), ())))

    enter(coarse, quarters, c_src, c_weight, c_scaled)
    for step in range(SWEEPS - 1):
        sweep(coarse, step, c_weight, c_scaled, coarse.nx)
    for x in range(coarse.nx):
        c_out[x] = c_fields[last, x + 1][:, :cells]
    store_coarse = pltpu.make_async_copy(c_out, coarse_hbm, local_sem.at[7])
    store_coarse.start()
    coarse.wait_yz(last)
    coarse.wait_x(last)
    valid = lax.broadcasted_iota(jnp.int32, (coarse.ny, LANES), 1) < cells
    for x in range(coarse.nx):
        value, around = coarse.around(last, x)
        part = c_src[x] - ((6.0 + c_damp[x]) * value - around)
        c_defect[pl.ds(x * coarse.ny, coarse.ny), :] = jnp.where(valid, part, 0.0)

    packed = c_defect[pl.ds(0, rows // 2), :]
    packed = packed + pltpu.roll(c_defect[pl.ds(rows // 2, rows // 2), :], cells, 1)
    c_defect[pl.ds(0, rows // 2), :] = packed

    tall = NAGG // LANES

    def gather_row(row, total):
        number = lax.broadcasted_iota(jnp.int32, (tall, LANES), 0)
        parts = []
        for part in range(2):
            at = pl.ds(row + part * half, 1)
            high = group_rows[at, :] // LANES
            parts.append(jnp.where(number == high, c_defect[at, :], 0.0))
        values = jnp.concatenate(parts, axis=1)
        first = values.astype(jnp.bfloat16).astype(jnp.float32)
        both = jnp.concatenate([first, values - first], axis=0).astype(jnp.bfloat16)
        return total + lax.dot_general(both, onehot[row], (((1,), (1,)), ((), ())),
                                       preferred_element_type=jnp.float32)

    sums = lax.fori_loop(0, half, gather_row, jnp.zeros((2 * tall, LANES), jnp.float32))
    mine = gx * cz + gz
    reduced[mine] = sums[:tall] + sums[tall:]

    def reduce_copy(i, k):
        return pltpu.make_async_remote_copy(
            src_ref=reduced.at[mine], dst_ref=reduced.at[mine],
            send_sem=r_send.at[i * cz + k], recv_sem=r_recv.at[mine],
            device_id=(i, gy, k), device_id_type=MESH)

    def reduce_wait(i, k):
        return pltpu.make_async_remote_copy(
            src_ref=reduced.at[i * cz + k], dst_ref=reduced.at[i * cz + k],
            send_sem=r_send.at[i * cz + k], recv_sem=r_recv.at[i * cz + k],
            device_id=(i, gy, k), device_id_type=MESH)

    def mates_do(act):
        for i, k in mates:
            pl.when(jnp.logical_or(gx != i, gz != k))(functools.partial(act, i, k))

    mates_do(lambda i, k: reduce_copy(i, k).start())
    mates_do(lambda i, k: reduce_wait(i, k).wait_recv())
    gathered[gy] = jnp.sum(reduced[...], axis=0)

    def gather_copy(j, slot, recv):
        return pltpu.make_async_remote_copy(
            src_ref=gathered.at[slot], dst_ref=gathered.at[slot],
            send_sem=g_send.at[j], recv_sem=g_recv.at[recv],
            device_id=(gx, j, gz), device_id_type=MESH)

    for j in range(cy):
        pl.when(gy != j)(lambda j=j: gather_copy(j, gy, gy).start())
    for j in range(cy):
        pl.when(gy != j)(lambda j=j: gather_copy(j, j, j).wait_recv())
    total_cells = rows * cells * cx * cy * cz
    source = jnp.sum(gathered[...], axis=0) * (1.0 / math.sqrt(total_cells // NAGG))

    loads[4].wait()
    out_rows = inverse.shape[0]
    product = None
    for part in range(tall):
        term = inverse[:, part * LANES:(part + 1) * LANES] * source[part:part + 1]
        product = term if product is None else product + term
    ones = jnp.ones((8, LANES), jnp.float32)
    solved = lax.dot_general(ones, product, (((1,), (1,)), ((), ())),
                             precision=lax.Precision.HIGHEST, preferred_element_type=jnp.float32)
    solved_ref[...] = solved[0:1]

    for step in range(SWEEPS + 1):
        if step == 0:
            fine.wait_send(first_x)
            fine.wait_send(fine.y_copies(0))
            fine.z_copy(0).wait_send()
        else:
            fine.wait_sends(step)
    for step in range(SWEEPS):
        middle.wait_sends(step)
        coarse.wait_sends(step)
    mates_do(lambda i, k: reduce_copy(i, k).wait_send())
    for j in range(cy):
        pl.when(gy != j)(lambda j=j: gather_copy(j, gy, gy).wait_send())
    store_fine.wait()
    store_middle.wait()
    store_coarse.wait()


def shards(counts, right_side, initial_guess, damping, group_map, block_inverse):
    bx, by, bz = right_side.shape
    f32 = jnp.float32
    vm = pltpu.VMEM

    def level_scratch(nx, ny, lanes, rounds):
        return [
            vm((rounds, nx + 2, ny, lanes), f32),
            vm((rounds, 2, nx, lanes), f32), vm((rounds, 2, nx, lanes), f32),
            vm((rounds, ny, LANES), f32), vm((rounds, ny, LANES), f32),
        ]

    cx, cy, cz = counts
    mid = (bx // 2, by // 2, bz // 2)
    low = (bx // 4, by // 4, bz // 4)
    low_pad = (low[0], low[1], LANES)
    rows = low[0] * low[1]
    out_rows = block_inverse.shape[0]
    dma = pltpu.SemaphoreType.DMA
    any_space = pl.BlockSpec(memory_space=pl.ANY)
    outs = pl.pallas_call(
        functools.partial(kernel, counts),
        out_shape=(
            jax.ShapeDtypeStruct((bx, by, bz), f32),
            jax.ShapeDtypeStruct(mid, f32),
            jax.ShapeDtypeStruct(low, f32),
            jax.ShapeDtypeStruct((1, out_rows), f32),
        ),
        in_specs=[any_space] * 5,
        out_specs=(any_space, any_space, any_space, pl.BlockSpec(memory_space=pltpu.VMEM)),
        scratch_shapes=[
            *level_scratch(bx, by, bz, SWEEPS + 1),
            *level_scratch(*mid, SWEEPS),
            *level_scratch(*low_pad, SWEEPS),
            vm((bx, by, bz), f32), vm((bx, by, bz), f32), vm(low, jnp.int32), vm(block_inverse.shape, f32),
            vm((bx, by, bz), f32), vm((bx, by, bz), f32),
            vm(mid, f32), vm(mid, f32), vm(mid, f32), vm(mid, f32),
            vm(low_pad, f32), vm(low_pad, f32), vm(low_pad, f32), vm(low_pad, f32),
            vm((mid[0] * by, LANES), f32), vm((low[0] * mid[1], LANES), f32),
            vm((rows, LANES), f32), vm(low, f32), vm((rows, LANES), jnp.int32),
            vm((rows // 4, LANES, 2 * LANES), jnp.bfloat16),
            vm((cx * cz, NAGG // LANES, LANES), f32), vm((cy, NAGG // LANES, LANES), f32),
            dma((SWEEPS + 1, 5)), dma((SWEEPS + 1, 5)),
            dma((SWEEPS, 5)), dma((SWEEPS, 5)), dma((SWEEPS, 5)), dma((SWEEPS, 5)),
            dma((cx * cz,)), dma((cx * cz,)), dma((cy,)), dma((cy,)), dma((8,)),
        ],
        compiler_params=pltpu.CompilerParams(
            collective_id=0, has_side_effects=True, vmem_limit_bytes=48 * 1024 * 1024),
        cost_estimate=pl.CostEstimate(flops=40_000_000, bytes_accessed=6_000_000, transcendentals=0),
    )(right_side, initial_guess, damping, group_map, block_inverse)
    fine, middle, coarse, solved = outs
    return fine, middle, coarse, solved.reshape(out_rows)


def solution(mesh):
    counts = tuple(mesh.shape[axis] for axis in ("gx", "gy", "gz"))
    cells = P("gx", "gy", "gz")
    return jax.shard_map(
        functools.partial(shards, counts),
        mesh=mesh,
        in_specs=(cells, cells, cells, cells, P("gy", None)),
        out_specs=(cells, cells, cells, P("gy")),
        check_vma=False,
    )
```

time: 762 us -> 82.8 us (0.11); the launches traced: 751 us -> 82.5 us
  local copies, waits for them, and re-layouts: 245 us -> 8.45 us
  starting transfers between devices: 187 us -> 0 us
  other arithmetic: 172 us -> 0 us
  waiting for transfers between devices: 103 us -> 0 us
  Pallas kernels: 0 us -> 73.3 us
  blocking collectives: 40.3 us -> 0 us
    ppermute x78 -> x0, starting transfers between devices: 187 us -> none  [the longest x39 136 us: with_halo(): lax.ppermute(tail, axis, [(i, (i + 1) % count) for i in range(ends)])]
    reshape x4 -> x0, local copies, waits for them, and re-layouts: 147 us -> none  [the longest x3 147 us: shrink(): blocks = field.reshape(extent_a // 2, 2, extent_b // 2, 2, extent_c // 2, 2)]
    ppermute x78 -> x0, waiting for transfers between devices: 103 us -> none  [the longest x39 79.7 us: with_halo(): lax.ppermute(head, axis, [((i + 1) % count, i) for i in range(ends)])]
    pallas_call x0 -> x1, Pallas kernels: none -> 73.3 us  [shards(): pl.pallas_call(functools.partial(kernel, counts), out_shape=(jax.ShapeDty...]
    add x10 -> x0, other arithmetic: 52.4 us -> none  [relax(): centre + OMEGA * (source - (diagonal * centre - neighbours(padded))) / di...]
    reduce_sum x4 -> x0, other arithmetic: 49.6 us -> none  [shrink(): return blocks.sum(axis=(1, 3, 5)) * 0.125]
    psum x1 -> x0, blocking collectives: 40.3 us -> none  [shards(): summed = lax.psum(partial_sums, ('gx', 'gy', 'gz'))]
    slice x42 -> x0, local copies, waits for them, and re-layouts: 37.7 us -> none  [the longest x25 25.5 us: with_halo(): lax.slice_in_dim(cells, cells.shape[dim] - width, cells.shape[dim], axis=...]
  transfers between devices with their start and end apart: 78 -> 0, of which waited for: 48 -> 0; matrix products, arithmetic and copies ran while one was open for 19% -> 0% of each run, Pallas kernels for 0% -> 0%
where the time goes in v1:
time: 82.8 us; the launch traced here: 82.5 us
  Pallas kernels  73.3 us (89%)
  local copies, waits for them, and re-layouts  8.45 us (10%)
    pallas_call x1, Pallas kernels, shards(): pl.pallas_call(functools.partial(kernel, counts), out_shape=(jax.ShapeDty...  73.3 us
    unnamed x14, local copies, waits for them, and re-layouts  8.45 us

profile of v1, /device:TPU:0, one launch (start us, length us, event | category | flops | bytes accessed | tf_op | source)
XLA Modules:
  0.0 82.5 jit_solution(4922080085546430436)
XLA Ops:
  0.6 0.0 copy-start
  0.6 1.2 %copy-done = f32[16,64,256]{2,1,0:T(8,128)S(1)} copy-done((f32[16,64,256]{2,1,0:T(8,128)S(1)}, f32[16,64,256]{2,1,0:T(8,128)}, u32[]{:S(2)}) %copy-start) | copy-done | bytes 1048600
  1.9 0.0 copy-start.1
  1.9 1.2 %copy-done.1 = f32[16,64,256]{2,1,0:T(8,128)S(1)} copy-done((f32[16,64,256]{2,1,0:T(8,128)S(1)}, f32[16,64,256]{2,1,0:T(8,128)}, u32[]{:S(2)}) %copy-start.1) | copy-done | bytes 1048600
  3.1 0.0 copy-start.2
  3.1 1.2 %copy-done.2 = f32[16,64,256]{2,1,0:T(8,128)S(1)} copy-done((f32[16,64,256]{2,1,0:T(8,128)S(1)}, f32[16,64,256]{2,1,0:T(8,128)}, u32[]{:S(2)}) %copy-start.2) | copy-done | bytes 1048600
  4.3 0.0 copy-start.3
  4.3 1.2 %copy-done.3 = f32[256,1024]{1,0:T(8,128)S(1)} copy-done((f32[256,1024]{1,0:T(8,128)S(1)}, f32[256,1024]{1,0:T(8,128)}, u32[]{:S(2)}) %copy-start.3) | copy-done | bytes 1048600
  5.5 0.0 copy-start.4
  5.5 0.8 copy-done.4
  6.3 73.3 %shard_map.84 = (f32[16,64,256]{2,1,0:T(8,128)S(1)}, f32[8,32,128]{2,1,0:T(8,128)S(1)}, f32[4,16,64]{2,1,0:T(8,128)S(1)}, f32[1,256]{1,0:T(1,128)S(1)}) custom-call(f32[16,64,256]{2,1,0:T(8,128)S(1)} %copy-done, f32[16,64,256]{2,1,0:T(8,128)S(1)} %copy-done.1, f32[16,64,256]{2,1,0:T(8,128)S(1)} %copy-done.2, s32[4,16,64]{2,1,0:T(8,128)S(1)} %copy-done.4, ...), custom_call_target="tpu_custom_call" | custom-call | flops 40000000 | bytes 6000000 | tf_op jit(solution)/shard_map/pallas_call | solution.py:463
  79.6 1.0 %copy.13 = f32[16,64,256]{2,1,0:T(8,128)} copy(f32[16,64,256]{2,1,0:T(8,128)S(1)} %get-tuple-element.16) | data formatting | bytes 2097152
  80.6 0.7 copy.14
  81.3 0.6 copy.15
  81.9 0.6 copy.16
Async XLA Ops:
  0.6 1.2 %copy-start = (f32[16,64,256]{2,1,0:T(8,128)S(1)}, f32[16,64,256]{2,1,0:T(8,128)}, u32[]{:S(2)}) copy-start(f32[16,64,256]{2,1,0:T(8,128)} %rhs_hbm.1) | copy-start | bytes 3145732
  1.9 1.2 %copy-start.1 = (f32[16,64,256]{2,1,0:T(8,128)S(1)}, f32[16,64,256]{2,1,0:T(8,128)}, u32[]{:S(2)}) copy-start(f32[16,64,256]{2,1,0:T(8,128)} %guess_hbm.1) | copy-start | bytes 3145732
  3.1 1.2 %copy-start.2 = (f32[16,64,256]{2,1,0:T(8,128)S(1)}, f32[16,64,256]{2,1,0:T(8,128)}, u32[]{:S(2)}) copy-start(f32[16,64,256]{2,1,0:T(8,128)} %damp_hbm.1) | copy-start | bytes 3145732
  4.3 1.2 %copy-start.3 = (f32[256,1024]{1,0:T(8,128)S(1)}, f32[256,1024]{1,0:T(8,128)}, u32[]{:S(2)}) copy-start(f32[256,1024]{1,0:T(8,128)} %inverse_hbm.1) | copy-start | bytes 3145732
  5.5 0.8 copy-start.4

commit v2 on v1

--- a/solution.py
+++ b/solution.py
@@ -42,17 +42,17 @@
 
     def clear(self):
         nx, ny, lanes = self.nx, self.ny, self.lanes
-        rounds = self.fields.shape[0]
+        rounds = len(self.fields)
 
         @pl.when(self.gx == 0)
         def _():
             for step in range(rounds):
-                self.fields[step, 0] = jnp.zeros((ny, lanes), jnp.float32)
+                self.fields[step][0] = jnp.zeros((ny, lanes), jnp.float32)
 
         @pl.when(self.gx == self.counts[0] - 1)
         def _():
             for step in range(rounds):
-                self.fields[step, nx + 1] = jnp.zeros((ny, lanes), jnp.float32)
+                self.fields[step][nx + 1] = jnp.zeros((ny, lanes), jnp.float32)
 
         @pl.when(self.gy == 0)
         def _():
@@ -69,7 +69,7 @@
 
     def x_copies(self, step, low=None, high=None):
         gx, gy, gz = self.gx, self.gy, self.gz
-        field = self.fields.at[step]
+        field = self.fields[step]
         low = field.at[1] if low is None else low
         high = field.at[self.nx] if high is None else high
         up = pltpu.make_async_remote_copy(
@@ -138,7 +138,7 @@
         self.wait_send(self.y_copies(step))
         self.z_copy(step).wait_send()
 
-    def pack(self, step, x, value):
+    def pack(self, step, x, value, face):
         ny, lanes = self.ny, self.lanes
         self.y_send[step, 0, pl.ds(x, 1), :] = value[0:1]
         self.y_send[step, 1, pl.ds(x, 1), :] = value[ny - 1:ny]
@@ -149,26 +149,34 @@
         edge = lax.rem(self.edge, LANES)
         turned = pltpu.roll(tile, lax.rem(x - edge + LANES, LANES), 1)
         lane = lax.broadcasted_iota(jnp.int32, (ny, LANES), 1)
-        self.z_send[step] = jnp.where(lane == x, turned, self.z_send[step])
+        return jnp.where(lane == x, turned, face)
 
     def around(self, step, x):
         ny, lanes = self.ny, self.lanes
-        field = self.fields.at[step]
+        field = self.fields[step]
         value = field[x + 1]
-        total = field[x] + field[x + 2]
-        row = lax.broadcasted_iota(jnp.int32, (ny, lanes), 0)
-        lane = lax.broadcasted_iota(jnp.int32, (ny, lanes), 1)
         below = self.y_recv[step, 0, pl.ds(x, 1), :]
         above = self.y_recv[step, 1, pl.ds(x, 1), :]
-        total = total + jnp.where(row == 0, below, pltpu.roll(value, 1, 0))
-        total = total + jnp.where(row == ny - 1, above, pltpu.roll(value, ny - 1, 0))
-        total = total + jnp.where(lane == 0, 0.0, pltpu.roll(value, 1, 1))
-        total = total + jnp.where(lane == lanes - 1, 0.0, pltpu.roll(value, lanes - 1, 1))
-        edge = lax.rem(self.edge, LANES)
-        face = pltpu.roll(self.z_recv[step], lax.rem(edge - x + LANES, LANES), 1)
-        if lanes > LANES:
-            face = jnp.concatenate([face] * (lanes // LANES), axis=1)
-        return value, total + jnp.where(lane == self.edge, face, 0.0)
+        total = field[x] + field[x + 2]
+        total = total + jnp.concatenate([below, value[:ny - 1]], axis=0)
+        total = total + jnp.concatenate([value[1:], above], axis=0)
+        lane = lax.broadcasted_iota(jnp.int32, (ny, LANES), 1)
+        face = pltpu.roll(self.z_recv[step], lax.rem(lax.rem(self.edge, LANES) - x + LANES, LANES), 1)
+        left_face = jnp.where(self.gz == 0, 0.0, face)
+        right_face = jnp.where(self.gz == 0, face, 0.0)
+        tiles = [value[:, at:at + LANES] for at in range(0, lanes, LANES)]
+        lefts = [left_face] + [pltpu.roll(tile, 1, 1) for tile in tiles]
+        rights = [pltpu.roll(tile, LANES - 1, 1) for tile in tiles] + [right_face]
+        sides = []
+        for at in range(len(tiles)):
+            right = rights[at]
+            if at + 1 < len(tiles) or self.nz == lanes:
+                right = jnp.where(lane == LANES - 1, rights[at + 1], right)
+            else:
+                right = jnp.where(lane == self.nz - 1, right_face, right)
+            sides.append(jnp.where(lane == 0, lefts[at], lefts[at + 1]) + right)
+        around = sides[0] if len(sides) == 1 else jnp.concatenate(sides, axis=1)
+        return value, total + around
 
 
 def kernel(counts, rhs_hbm, guess_hbm, damp_hbm, group_hbm, inverse_hbm,
@@ -191,7 +199,7 @@
                    (c_send, c_recv), place, counts)
 
     loads = [
-        pltpu.make_async_copy(guess_hbm, f_fields.at[0, pl.ds(1, bx)], local_sem.at[0]),
+        pltpu.make_async_copy(guess_hbm, f_fields[0].at[pl.ds(1, bx)], local_sem.at[0]),
         pltpu.make_async_copy(damp_hbm, damp, local_sem.at[1]),
         pltpu.make_async_copy(rhs_hbm, rhs, local_sem.at[2]),
         pltpu.make_async_copy(group_hbm, group, local_sem.at[3]),
@@ -219,9 +227,13 @@
     fine.start(first_x)
     loads[0].wait()
 
-    @pl.loop(0, bx)
-    def _(x):
-        fine.pack(0, x, f_fields[0, x + 1])
+    @pl.loop(0, bx // 4)
+    def _(group):
+        face = f_zs[0]
+        for part in range(4):
+            x = group * 4 + part
+            face = fine.pack(0, x, f_fields[0][x + 1], face)
+        f_zs[0] = face
 
     fine.start_yz(0)
 
@@ -230,7 +242,7 @@
     pair_fine = pair_matrix(bz, bz // 2)
     pair_middle = pair_matrix(bz // 2, LANES)
 
-    @pl.loop(0, bx)
+    @pl.loop(0, bx, unroll=4)
     def _(x):
         factor = OMEGA / (6.0 + damp[x])
         weight[x] = factor
@@ -262,7 +274,7 @@
     group_rows[pl.ds(0, rows // 2), :] = packed
     half = rows // 4
 
-    @pl.loop(0, half)
+    @pl.loop(0, half, unroll=4)
     def _(row):
         number = lax.broadcasted_iota(jnp.int32, (LANES, LANES), 0)
         for part in range(2):
@@ -270,27 +282,39 @@
             onehot[row, :, part * LANES:(part + 1) * LANES] = jnp.where(
                 number == low, 1.0, 0.0).astype(jnp.bfloat16)
 
-    def sweep(level, step, weights, scaleds, planes, unroll=1):
-        def one(x):
+    def sweep(level, step, weights, scaleds, planes):
+        def one(x, face):
             value, total = level.around(step, x)
             new = (1.0 - OMEGA) * value + (scaleds[x] + weights[x] * total)
-            level.fields[step + 1, x + 1] = new
-            level.pack(step + 1, x, new)
+            level.fields[step + 1][x + 1] = new
+            return level.pack(step + 1, x, new, face)
 
         level.wait_yz(step)
-
-        @pl.loop(1, planes - 1)
-        def _(x):
-            one(x)
+        size = 2 if planes > 8 else planes - 2
+
+        def some(first):
+            face = level.z_send[step + 1]
+            for part in range(size):
+                face = one(first + part, face)
+            level.z_send[step + 1] = face
+
+        if size == planes - 2:
+            some(1)
+        else:
+            @pl.loop(0, (planes - 2) // size)
+            def _(group):
+                some(group * size + 1)
 
         level.wait_x(step)
-        one(0)
-        one(planes - 1)
-        level.start_all(step + 1)
+        face = one(0, level.z_send[step + 1])
+        face = one(planes - 1, face)
+        level.start(level.x_copies(step + 1))
+        level.z_send[step + 1] = face
+        level.start_yz(step + 1)
 
     for step in range(SWEEPS):
         sweep(fine, step, weight, scaled, bx)
-    store_fine = pltpu.make_async_copy(f_fields.at[SWEEPS, pl.ds(1, bx)], fine_hbm, local_sem.at[5])
+    store_fine = pltpu.make_async_copy(f_fields[SWEEPS].at[pl.ds(1, bx)], fine_hbm, local_sem.at[5])
     store_fine.start()
 
     fine.wait_yz(SWEEPS)
@@ -303,7 +327,7 @@
             total = part if total is None else total + part
         halves[pl.ds(pl.multiple_of(x * by, by), by), :] = split_dot(total, pair_fine, (((1,), (0,)), ((), ())))
 
-    @pl.loop(1, middle.nx - 1)
+    @pl.loop(1, middle.nx - 1, unroll=2)
     def _(x):
         defect_pair(x)
 
@@ -313,20 +337,23 @@
 
     def enter(level, scratch, source, weights, scaleds):
         ny = level.ny
+        face = jnp.zeros((ny, LANES), jnp.float32)
         for x in range(level.nx):
             even = scratch[pl.ds(x * 2 * ny, ny, stride=2), :]
             odd = scratch[pl.ds(x * 2 * ny + 1, ny, stride=2), :]
             source[x] = 0.5 * (even + odd)
-            scaleds[x] = weights[x] * source[x]
-            level.fields[0, x + 1] = scaleds[x]
-            level.pack(0, x, scaleds[x])
+            new = weights[x] * source[x]
+            scaleds[x] = new
+            level.fields[0][x + 1] = new
+            face = level.pack(0, x, new, face)
+        level.z_send[0] = face
         level.start_all(0)
 
     enter(middle, halves, m_src, m_weight, m_scaled)
     for step in range(SWEEPS - 1):
         sweep(middle, step, m_weight, m_scaled, middle.nx)
     last = SWEEPS - 1
-    store_middle = pltpu.make_async_copy(m_fields.at[last, pl.ds(1, middle.nx)], middle_hbm, local_sem.at[6])
+    store_middle = pltpu.make_async_copy(m_fields[last].at[pl.ds(1, middle.nx)], middle_hbm, local_sem.at[6])
     store_middle.start()
     middle.wait_yz(last)
     middle.wait_x(last)
@@ -344,7 +371,7 @@
     for step in range(SWEEPS - 1):
         sweep(coarse, step, c_weight, c_scaled, coarse.nx)
     for x in range(coarse.nx):
-        c_out[x] = c_fields[last, x + 1][:, :cells]
+        c_out[x] = c_fields[last][x + 1][:, :cells]
     store_coarse = pltpu.make_async_copy(c_out, coarse_hbm, local_sem.at[7])
     store_coarse.start()
     coarse.wait_yz(last)
@@ -374,7 +401,8 @@
         return total + lax.dot_general(both, onehot[row], (((1,), (1,)), ((), ())),
                                        preferred_element_type=jnp.float32)
 
-    sums = lax.fori_loop(0, half, gather_row, jnp.zeros((2 * tall, LANES), jnp.float32))
+    sums = lax.fori_loop(0, half, gather_row, jnp.zeros((2 * tall, LANES), jnp.float32),
+                         unroll=4)
     mine = gx * cz + gz
     reduced[mine] = sums[:tall] + sums[tall:]
 
@@ -447,7 +475,7 @@
 
     def level_scratch(nx, ny, lanes, rounds):
         return [
-            vm((rounds, nx + 2, ny, lanes), f32),
+            [vm((nx + 2, ny, lanes), f32)] * rounds,
             vm((rounds, 2, nx, lanes), f32), vm((rounds, 2, nx, lanes), f32),
             vm((rounds, ny, LANES), f32), vm((rounds, ny, LANES), f32),
         ]
@@ -460,6 +488,7 @@
     out_rows = block_inverse.shape[0]
     dma = pltpu.SemaphoreType.DMA
     any_space = pl.BlockSpec(memory_space=pl.ANY)
+    in_hbm = pl.BlockSpec(memory_space=pltpu.HBM)
     outs = pl.pallas_call(
         functools.partial(kernel, counts),
         out_shape=(
@@ -468,7 +497,7 @@
             jax.ShapeDtypeStruct(low, f32),
             jax.ShapeDtypeStruct((1, out_rows), f32),
         ),
-        in_specs=[any_space] * 5,
+        in_specs=[in_hbm] * 5,
         out_specs=(any_space, any_space, any_space, pl.BlockSpec(memory_space=pltpu.VMEM)),
         scratch_shapes=[
             *level_scratch(bx, by, bz, SWEEPS + 1),

time: 82.8 us -> 73.1 us (0.88)
  Pallas kernels: 73.3 us -> 63.6 us
    pallas_call x1, Pallas kernels: 73.3 us -> 63.6 us  [shards(): pl.pallas_call(functools.partial(kernel, counts), out_shape=(jax.ShapeDty...]
where the time goes in v2:
time: 73.1 us; the launch traced here: 72.7 us
  Pallas kernels  63.6 us (87%)
  local copies, waits for them, and re-layouts  8.45 us (12%)
    pallas_call x1, Pallas kernels, shards(): pl.pallas_call(functools.partial(kernel, counts), out_shape=(jax.ShapeDty...  63.6 us
    unnamed x14, local copies, waits for them, and re-layouts  8.45 us

profile of v2, /device:TPU:0, one launch (start us, length us, event | category | flops | bytes accessed | tf_op | source)
XLA Modules:
  0.0 72.7 jit_solution(16306204087112346161)
XLA Ops:
  0.6 0.0 copy-start
  0.6 1.2 %copy-done = f32[16,64,256]{2,1,0:T(8,128)S(1)} copy-done((f32[16,64,256]{2,1,0:T(8,128)S(1)}, f32[16,64,256]{2,1,0:T(8,128)}, u32[]{:S(2)}) %copy-start) | copy-done | bytes 1048600
  1.9 0.0 copy-start.1
  1.9 1.2 %copy-done.1 = f32[16,64,256]{2,1,0:T(8,128)S(1)} copy-done((f32[16,64,256]{2,1,0:T(8,128)S(1)}, f32[16,64,256]{2,1,0:T(8,128)}, u32[]{:S(2)}) %copy-start.1) | copy-done | bytes 1048600
  3.1 0.0 copy-start.2
  3.1 1.2 %copy-done.2 = f32[16,64,256]{2,1,0:T(8,128)S(1)} copy-done((f32[16,64,256]{2,1,0:T(8,128)S(1)}, f32[16,64,256]{2,1,0:T(8,128)}, u32[]{:S(2)}) %copy-start.2) | copy-done | bytes 1048600
  4.3 0.0 copy-start.3
  4.3 1.2 %copy-done.3 = f32[256,1024]{1,0:T(8,128)S(1)} copy-done((f32[256,1024]{1,0:T(8,128)S(1)}, f32[256,1024]{1,0:T(8,128)}, u32[]{:S(2)}) %copy-start.3) | copy-done | bytes 1048600
  5.5 0.0 copy-start.4
  5.5 0.8 %copy-done.4 = s32[4,16,64]{2,1,0:T(8,128)S(1)} copy-done((s32[4,16,64]{2,1,0:T(8,128)S(1)}, s32[4,16,64]{2,1,0:T(8,128)}, u32[]{:S(2)}) %copy-start.4) | copy-done | bytes 16408
  6.3 63.6 %shard_map.84 = (f32[16,64,256]{2,1,0:T(8,128)S(1)}, f32[8,32,128]{2,1,0:T(8,128)S(1)}, f32[4,16,64]{2,1,0:T(8,128)S(1)}, f32[1,256]{1,0:T(1,128)S(1)}) custom-call(f32[16,64,256]{2,1,0:T(8,128)S(1)} %copy-done, f32[16,64,256]{2,1,0:T(8,128)S(1)} %copy-done.1, f32[16,64,256]{2,1,0:T(8,128)S(1)} %copy-done.2, s32[4,16,64]{2,1,0:T(8,128)S(1)} %copy-done.4, ...), custom_call_target="tpu_custom_call" | custom-call | flops 40000000 | bytes 6000000 | tf_op jit(solution)/shard_map/pallas_call | solution.py:492
  69.9 1.0 %copy.13 = f32[16,64,256]{2,1,0:T(8,128)} copy(f32[16,64,256]{2,1,0:T(8,128)S(1)} %get-tuple-element.16) | data formatting | bytes 2097152
  70.9 0.7 copy.14
  71.5 0.6 copy.15
  72.2 0.6 copy.16
Async XLA Ops:
  0.6 1.2 %copy-start = (f32[16,64,256]{2,1,0:T(8,128)S(1)}, f32[16,64,256]{2,1,0:T(8,128)}, u32[]{:S(2)}) copy-start(f32[16,64,256]{2,1,0:T(8,128)} %rhs_hbm.1) | copy-start | bytes 3145732
  1.9 1.2 %copy-start.1 = (f32[16,64,256]{2,1,0:T(8,128)S(1)}, f32[16,64,256]{2,1,0:T(8,128)}, u32[]{:S(2)}) copy-start(f32[16,64,256]{2,1,0:T(8,128)} %guess_hbm.1) | copy-start | bytes 3145732
  3.1 1.2 %copy-start.2 = (f32[16,64,256]{2,1,0:T(8,128)S(1)}, f32[16,64,256]{2,1,0:T(8,128)}, u32[]{:S(2)}) copy-start(f32[16,64,256]{2,1,0:T(8,128)} %damp_hbm.1) | copy-start | bytes 3145732
  4.3 1.2 %copy-start.3 = (f32[256,1024]{1,0:T(8,128)S(1)}, f32[256,1024]{1,0:T(8,128)}, u32[]{:S(2)}) copy-start(f32[256,1024]{1,0:T(8,128)} %inverse_hbm.1) | copy-start | bytes 3145732
  5.5 0.8 %copy-start.4 = (s32[4,16,64]{2,1,0:T(8,128)S(1)}, s32[4,16,64]{2,1,0:T(8,128)}, u32[]{:S(2)}) copy-start(s32[4,16,64]{2,1,0:T(8,128)} %group_hbm.1) | copy-start | bytes 49156

commit v3 on v2

--- a/solution.py
+++ b/solution.py
@@ -516,7 +516,7 @@
             dma((cx * cz,)), dma((cx * cz,)), dma((cy,)), dma((cy,)), dma((8,)),
         ],
         compiler_params=pltpu.CompilerParams(
-            collective_id=0, has_side_effects=True, vmem_limit_bytes=48 * 1024 * 1024),
+            collective_id=0, has_side_effects=True, vmem_limit_bytes=63 * 1024 * 1024),
         cost_estimate=pl.CostEstimate(flops=40_000_000, bytes_accessed=6_000_000, transcendentals=0),
     )(right_side, initial_guess, damping, group_map, block_inverse)
     fine, middle, coarse, solved = outs

time: 73.1 us -> 69.1 us (0.945)
  local copies, waits for them, and re-layouts: 8.45 us -> 4.33 us
    unnamed x14 -> x10, local copies, waits for them, and re-layouts: 8.45 us -> 4.33 us
where the time goes in v3:
time: 69.1 us; the launch traced here: 68.9 us
  Pallas kernels  63.9 us (92%)
  local copies, waits for them, and re-layouts  4.33 us (6%)
    pallas_call x1, Pallas kernels, shards(): pl.pallas_call(functools.partial(kernel, counts), out_shape=(jax.ShapeDty...  63.9 us
    unnamed x10, local copies, waits for them, and re-layouts  4.33 us

profile of v3, /device:TPU:0, one launch (start us, length us, event | category | flops | bytes accessed | tf_op | source)
XLA Modules:
  0.0 68.9 jit_solution(9651975869643417161)
XLA Ops:
  0.6 63.9 %shard_map.84 = (f32[16,64,256]{2,1,0:T(8,128)}, f32[8,32,128]{2,1,0:T(8,128)}, f32[4,16,64]{2,1,0:T(8,128)}, f32[1,256]{1,0:T(1,128)}) custom-call(f32[16,64,256]{2,1,0:T(8,128)} %rhs_hbm.1, f32[16,64,256]{2,1,0:T(8,128)} %guess_hbm.1, f32[16,64,256]{2,1,0:T(8,128)} %damp_hbm.1, s32[4,16,64]{2,1,0:T(8,128)} %group_hbm.1, f32[256,1024]{1,0:T(8,128)} %inverse_hbm.1), custom_call_target="tpu_custom_call" | custom-call | flops 40000000 | bytes 6000000 | tf_op jit(solution)/shard_map/pallas_call | solution.py:492
  64.6 0.0 copy-start
  64.6 2.3 %copy.13 = f32[16,64,256]{2,1,0:T(8,128)} copy(f32[16,64,256]{2,1,0:T(8,128)} %get-tuple-element.16) | data formatting | bytes 2097152
  66.9 0.0 copy-done
  66.9 0.0 copy-start.1
  66.9 0.7 copy.14
  67.6 0.1 copy-done.1
  67.7 0.0 copy-start.2
  67.7 0.6 copy.15
  68.3 0.1 copy-done.2
  68.3 0.6 copy.16
Async XLA Ops:
  64.6 2.3 %copy-start = (f32[8,32,128]{2,1,0:T(8,128)S(1)}, f32[8,32,128]{2,1,0:T(8,128)}, u32[]{:S(2)}) copy-start(f32[8,32,128]{2,1,0:T(8,128)} %get-tuple-element.17) | copy-start | bytes 393220
  66.9 0.8 %copy-start.1 = (f32[4,16,64]{2,1,0:T(8,128)S(1)}, f32[4,16,64]{2,1,0:T(8,128)}, u32[]{:S(2)}) copy-start(f32[4,16,64]{2,1,0:T(8,128)} %get-tuple-element.18) | copy-start | bytes 49156
  67.7 0.7 copy-start.2

commit v4 on v3

--- a/solution.py
+++ b/solution.py
@@ -12,6 +12,7 @@
 NAGG = 1024
 OMEGA = 0.8
 LANES = 128
+MARGIN = 8
 MESH = pl.DeviceIdType.MESH
 
 
@@ -179,15 +180,121 @@
         return value, total + around
 
 
+class Deep:
+    def __init__(self, dims, fields, wide, half, half_in, full, z_sems, d_sems, place, counts):
+        self.nx, self.ny, self.nz = dims
+        self.fields, self.wide = fields, wide
+        self.half, self.half_in, self.full = half, half_in, full
+        self.z_sems, self.d_sems = z_sems, d_sems
+        self.gx, self.gy, self.gz = place
+        self.counts = counts
+        self.ways = [(i, j) for i in (-1, 0, 1) for j in (-1, 0, 1) if (i, j) != (0, 0)]
+
+    def there(self, i, j):
+        here = jnp.bool_(True)
+        for at, count, step in ((self.gx, self.counts[0], i), (self.gy, self.counts[1], j)):
+            if step == 1:
+                here = jnp.logical_and(here, at < count - 1)
+            if step == -1:
+                here = jnp.logical_and(here, at > 0)
+        return here
+
+    def place_of(self, i, j):
+        low = {-1: 0, 0: MARGIN, 1: MARGIN + self.ny}[j]
+        return pl.ds((1 + i) * self.nx, self.nx), pl.ds(low, self.ny if j == 0 else MARGIN)
+
+    def corners(self):
+        beside = [jnp.where(self.there(i, j), 1, 0) for i, j in self.ways if i and j]
+        return sum(beside)
+
+    def greet(self, barrier):
+        for i, j in self.ways:
+            if i and j:
+                @pl.when(self.there(i, j))
+                def _():
+                    pl.semaphore_signal(barrier, inc=1, device_id=(self.gx + i, self.gy + j, self.gz),
+                                        device_id_type=MESH)
+
+    def clear(self):
+        for i, j in self.ways:
+            planes, rows = self.place_of(i, j)
+
+            @pl.when(jnp.logical_not(self.there(i, j)))
+            def _():
+                for kind in range(2):
+                    self.wide[kind, planes, rows, :] = jnp.zeros((planes.size, rows.size, LANES), jnp.float32)
+
+    def z_copy(self, kind):
+        return pltpu.make_async_remote_copy(
+            src_ref=self.half.at[kind], dst_ref=self.half_in.at[kind],
+            send_sem=self.z_sems[0].at[kind], recv_sem=self.z_sems[1].at[kind],
+            device_id=(self.gx, self.gy, 1 - self.gz), device_id_type=MESH)
+
+    def merge(self, kind, block):
+        for x in range(self.nx):
+            self.half[kind, x] = pltpu.roll(block[x], self.gz * self.nz, 1)
+        self.z_copy(kind).start()
+
+    def d_copy(self, kind, i, j):
+        planes, rows = self.place_of(-i, -j)
+        first = self.ny - MARGIN if j == 1 else 0
+        way = (i + 1) * 3 + j + 1
+        return pltpu.make_async_remote_copy(
+            src_ref=self.full.at[kind, :, pl.ds(first, rows.size)],
+            dst_ref=self.wide.at[kind, planes, rows],
+            send_sem=self.d_sems[0].at[kind, way], recv_sem=self.d_sems[1].at[kind, way],
+            device_id=(self.gx + i, self.gy + j, self.gz), device_id_type=MESH)
+
+    def spread(self, kind):
+        self.z_copy(kind).wait_recv()
+        self.full[kind] = self.half[kind] + self.half_in[kind]
+        for i, j in self.ways:
+            pl.when(self.there(i, j))(self.d_copy(kind, i, j).start)
+        planes, rows = self.place_of(0, 0)
+        self.wide[kind, planes, rows, :] = self.full[kind]
+
+    def collect(self, kind):
+        for i, j in self.ways:
+            pl.when(self.there(-i, -j))(self.d_copy(kind, i, j).wait_recv)
+
+    def wait_sends(self):
+        for kind in range(2):
+            self.z_copy(kind).wait_send()
+            for i, j in self.ways:
+                pl.when(self.there(i, j))(self.d_copy(kind, i, j).wait_send)
+
+    def own(self, plane):
+        return pltpu.roll(plane[MARGIN:MARGIN + self.ny], self.gz * self.nz, 1)
+
+    def around(self, step, x):
+        field = self.fields[step]
+        value = field[x]
+        rows = value.shape[0]
+        lane = lax.broadcasted_iota(jnp.int32, value.shape, 1)
+        total = field[x - 1] + field[x + 1]
+        total = total + pltpu.roll(value, 1, 0) + pltpu.roll(value, rows - 1, 0)
+        total = total + jnp.where(lane == 0, 0.0, pltpu.roll(value, 1, 1))
+        return value, total + jnp.where(lane == LANES - 1, 0.0, pltpu.roll(value, LANES - 1, 1))
+
+    def smooth(self):
+        planes = 3 * self.nx
+        for x in range(planes):
+            self.fields[0][x] = self.wide[0, x] * self.wide[1, x]
+        for step in range(1, SWEEPS):
+            for x in range(step, planes - step):
+                value, total = self.around(step - 1, x)
+                self.fields[step][x] = (1.0 - OMEGA) * value + self.wide[0, x] * (self.wide[1, x] + total)
+
+
 def kernel(counts, rhs_hbm, guess_hbm, damp_hbm, group_hbm, inverse_hbm,
            fine_hbm, middle_hbm, coarse_hbm, solved_ref,
            f_fields, f_ys, f_yr, f_zs, f_zr,
            m_fields, m_ys, m_yr, m_zs, m_zr,
-           c_fields, c_ys, c_yr, c_zs, c_zr,
+           c_fields, deep, half, half_in, full,
            rhs, damp, group, inverse, weight, scaled,
-           m_damp, m_src, m_weight, m_scaled, c_damp, c_src, c_weight, c_scaled,
+           m_damp, m_src, m_weight, m_scaled, c_damp, c_src,
            halves, quarters, c_defect, c_out, group_rows, onehot, reduced, gathered,
-           f_send, f_recv, m_send, m_recv, c_send, c_recv,
+           f_send, f_recv, m_send, m_recv, hz_send, hz_recv, d_send, d_recv,
            r_send, r_recv, g_send, g_recv, local_sem):
     place = gx, gy, gz = lax.axis_index("gx"), lax.axis_index("gy"), lax.axis_index("gz")
     cx, cy, cz = counts
@@ -195,8 +302,8 @@
     fine = Level((bx, by, bz), bz, f_fields, f_ys, f_yr, f_zs, f_zr, (f_send, f_recv), place, counts)
     middle = Level((bx // 2, by // 2, bz // 2), bz // 2, m_fields, m_ys, m_yr, m_zs, m_zr,
                    (m_send, m_recv), place, counts)
-    coarse = Level((bx // 4, by // 4, bz // 4), LANES, c_fields, c_ys, c_yr, c_zs, c_zr,
-                   (c_send, c_recv), place, counts)
+    coarse = Deep((bx // 4, by // 4, bz // 4), c_fields, deep, half, half_in, full,
+                  (hz_send, hz_recv), (d_send, d_recv), place, counts)
 
     loads = [
         pltpu.make_async_copy(guess_hbm, f_fields[0].at[pl.ds(1, bx)], local_sem.at[0]),
@@ -219,9 +326,10 @@
         def _():
             pl.semaphore_signal(barrier, inc=1, device_id=(gx, j, gz), device_id_type=MESH)
 
+    coarse.greet(barrier)
     for level in (fine, middle, coarse):
         level.clear()
-    pl.semaphore_wait(barrier, len(mates) - 1 + cy - 1)
+    pl.semaphore_wait(barrier, len(mates) - 1 + cy - 1 + coarse.corners())
 
     first_x = fine.x_copies(0, guess_hbm.at[0], guess_hbm.at[bx - 1])
     fine.start(first_x)
@@ -261,7 +369,7 @@
     shrink_to(lambda x: m_damp[x], c_damp, quarters, pair_middle, coarse.nx, coarse.ny)
     c_lane = lax.broadcasted_iota(jnp.int32, (coarse.nx, coarse.ny, LANES), 2)
     m_weight[...] = OMEGA / (6.0 + m_damp[...])
-    c_weight[...] = jnp.where(c_lane < coarse.nz, OMEGA / (6.0 + c_damp[...]), 0.0)
+    coarse.merge(0, jnp.where(c_lane < coarse.nz, OMEGA / (6.0 + c_damp[...]), 0.0))
 
     loads[3].wait()
     rows = coarse.nx * coarse.ny
@@ -314,6 +422,8 @@
 
     for step in range(SWEEPS):
         sweep(fine, step, weight, scaled, bx)
+        if step == 0:
+            coarse.spread(0)
     store_fine = pltpu.make_async_copy(f_fields[SWEEPS].at[pl.ds(1, bx)], fine_hbm, local_sem.at[5])
     store_fine.start()
 
@@ -367,19 +477,23 @@
             total = part if total is None else total + part
         quarters[pl.ds(x * my, my), :] = split_dot(total, pair_middle, (((1,), (0,)), ((), ())))
 
-    enter(coarse, quarters, c_src, c_weight, c_scaled)
-    for step in range(SWEEPS - 1):
-        sweep(coarse, step, c_weight, c_scaled, coarse.nx)
     for x in range(coarse.nx):
-        c_out[x] = c_fields[last][x + 1][:, :cells]
+        even = quarters[pl.ds(x * my, coarse.ny, stride=2), :]
+        odd = quarters[pl.ds(x * my + 1, coarse.ny, stride=2), :]
+        c_src[x] = 0.5 * (even + odd)
+    coarse.merge(1, c_src[...])
+    coarse.spread(1)
+    coarse.collect(0)
+    coarse.collect(1)
+    coarse.smooth()
+    for x in range(coarse.nx):
+        c_out[x] = coarse.own(c_fields[last][coarse.nx + x])[:, :cells]
     store_coarse = pltpu.make_async_copy(c_out, coarse_hbm, local_sem.at[7])
     store_coarse.start()
-    coarse.wait_yz(last)
-    coarse.wait_x(last)
     valid = lax.broadcasted_iota(jnp.int32, (coarse.ny, LANES), 1) < cells
     for x in range(coarse.nx):
-        value, around = coarse.around(last, x)
-        part = c_src[x] - ((6.0 + c_damp[x]) * value - around)
+        value, around = coarse.around(last, coarse.nx + x)
+        part = c_src[x] - ((6.0 + c_damp[x]) * coarse.own(value) - coarse.own(around))
         c_defect[pl.ds(x * coarse.ny, coarse.ny), :] = jnp.where(valid, part, 0.0)
 
     packed = c_defect[pl.ds(0, rows // 2), :]
@@ -459,7 +573,7 @@
             fine.wait_sends(step)
     for step in range(SWEEPS):
         middle.wait_sends(step)
-        coarse.wait_sends(step)
+    coarse.wait_sends()
     mates_do(lambda i, k: reduce_copy(i, k).wait_send())
     for j in range(cy):
         pl.when(gy != j)(lambda j=j: gather_copy(j, gy, gy).wait_send())
@@ -484,6 +598,7 @@
     mid = (bx // 2, by // 2, bz // 2)
     low = (bx // 4, by // 4, bz // 4)
     low_pad = (low[0], low[1], LANES)
+    wide = (3 * low[0], low[1] + 2 * MARGIN, LANES)
     rows = low[0] * low[1]
     out_rows = block_inverse.shape[0]
     dma = pltpu.SemaphoreType.DMA
@@ -502,17 +617,18 @@
         scratch_shapes=[
             *level_scratch(bx, by, bz, SWEEPS + 1),
             *level_scratch(*mid, SWEEPS),
-            *level_scratch(*low_pad, SWEEPS),
+            [vm(wide, f32)] * SWEEPS, vm((2, *wide), f32),
+            vm((2, *low_pad), f32), vm((2, *low_pad), f32), vm((2, *low_pad), f32),
             vm((bx, by, bz), f32), vm((bx, by, bz), f32), vm(low, jnp.int32), vm(block_inverse.shape, f32),
             vm((bx, by, bz), f32), vm((bx, by, bz), f32),
             vm(mid, f32), vm(mid, f32), vm(mid, f32), vm(mid, f32),
-            vm(low_pad, f32), vm(low_pad, f32), vm(low_pad, f32), vm(low_pad, f32),
+            vm(low_pad, f32), vm(low_pad, f32),
             vm((mid[0] * by, LANES), f32), vm((low[0] * mid[1], LANES), f32),
             vm((rows, LANES), f32), vm(low, f32), vm((rows, LANES), jnp.int32),
             vm((rows // 4, LANES, 2 * LANES), jnp.bfloat16),
             vm((cx * cz, NAGG // LANES, LANES), f32), vm((cy, NAGG // LANES, LANES), f32),
             dma((SWEEPS + 1, 5)), dma((SWEEPS + 1, 5)),
-            dma((SWEEPS, 5)), dma((SWEEPS, 5)), dma((SWEEPS, 5)), dma((SWEEPS, 5)),
+            dma((SWEEPS, 5)), dma((SWEEPS, 5)), dma((2,)), dma((2,)), dma((2, 9)), dma((2, 9)),
             dma((cx * cz,)), dma((cx * cz,)), dma((cy,)), dma((cy,)), dma((8,)),
         ],
         compiler_params=pltpu.CompilerParams(

time: 69.1 us -> 64 us (0.926)
  Pallas kernels: 63.9 us -> 58.8 us
    pallas_call x1, Pallas kernels: 63.9 us -> 58.8 us  [shards(): pl.pallas_call(functools.partial(kernel, counts), out_shape=(jax.ShapeDty...]
where the time goes in v4:
time: 64 us; the launch traced here: 63.8 us
  Pallas kernels  58.8 us (92%)
  local copies, waits for them, and re-layouts  4.33 us (7%)
  between operations  0.65 us (1%)
    pallas_call x1, Pallas kernels, shards(): pl.pallas_call(functools.partial(kernel, counts), out_shape=(jax.ShapeDty...  58.8 us
    unnamed x10, local copies, waits for them, and re-layouts  4.33 us

profile of v4, /device:TPU:0, one launch (start us, length us, event | category | flops | bytes accessed | tf_op | source)
XLA Modules:
  0.0 63.8 jit_solution(14007774643343519627)
XLA Ops:
  0.6 58.8 %shard_map.84 = (f32[16,64,256]{2,1,0:T(8,128)}, f32[8,32,128]{2,1,0:T(8,128)}, f32[4,16,64]{2,1,0:T(8,128)}, f32[1,256]{1,0:T(1,128)}) custom-call(f32[16,64,256]{2,1,0:T(8,128)} %rhs_hbm.1, f32[16,64,256]{2,1,0:T(8,128)} %guess_hbm.1, f32[16,64,256]{2,1,0:T(8,128)} %damp_hbm.1, s32[4,16,64]{2,1,0:T(8,128)} %group_hbm.1, f32[256,1024]{1,0:T(8,128)} %inverse_hbm.1), custom_call_target="tpu_custom_call" | custom-call | flops 40000000 | bytes 6000000 | tf_op jit(solution)/shard_map/pallas_call | solution.py:607
  59.5 0.0 copy-start
  59.5 2.3 %copy.13 = f32[16,64,256]{2,1,0:T(8,128)} copy(f32[16,64,256]{2,1,0:T(8,128)} %get-tuple-element.16) | data formatting | bytes 2097152
  61.8 0.0 copy-done
  61.8 0.0 copy-start.1
  61.8 0.7 %copy.14 = f32[8,32,128]{2,1,0:T(8,128)} copy(f32[8,32,128]{2,1,0:T(8,128)S(1)} %copy-done) | data formatting | bytes 262144
  62.5 0.1 copy-done.1
  62.6 0.0 copy-start.2
  62.6 0.6 copy.15
  63.2 0.1 copy-done.2
  63.3 0.6 copy.16
Async XLA Ops:
  59.5 2.3 %copy-start = (f32[8,32,128]{2,1,0:T(8,128)S(1)}, f32[8,32,128]{2,1,0:T(8,128)}, u32[]{:S(2)}) copy-start(f32[8,32,128]{2,1,0:T(8,128)} %get-tuple-element.17) | copy-start | bytes 393220
  61.8 0.8 %copy-start.1 = (f32[4,16,64]{2,1,0:T(8,128)S(1)}, f32[4,16,64]{2,1,0:T(8,128)}, u32[]{:S(2)}) copy-start(f32[4,16,64]{2,1,0:T(8,128)} %get-tuple-element.18) | copy-start | bytes 49156
  62.6 0.7 %copy-start.2 = (f32[1,256]{1,0:T(1,128)S(1)}, f32[1,256]{1,0:T(1,128)}, u32[]{:S(2)}) copy-start(f32[1,256]{1,0:T(1,128)} %get-tuple-element.11) | copy-start | bytes 3076
